TPU v7x, 32 devices: a whole 2x2x4 slice. The times are simulated.
32 devices in a mesh: groups: 2 (over x), ep: 16 (over z, y, core).
Axes of the slice: x: 2, y: 2, z: 4, core: 2. Of those that a mesh axis runs over, the one named last changes fastest.
Arguments:
- tokens: bfloat16 [2048, 2048], P(('groups', 'ep')), parts along dimension 0, may hold values from -6 to 6
- expert_ids: int32 [2048, 8], P(('groups', 'ep')), parts along dimension 0, may hold values from 0 to 15, as said below
- gate_values: float32 [2048, 8], P(('groups', 'ep')), parts along dimension 0, may hold values from 0.1 to 1
- expert_weights: bfloat16 [32, 2048, 3072], P(('groups', 'ep')), parts along dimension 0, as said below
- home_slot: int32 [32], P('groups'), parts along dimension 0, may hold values from 0 to 15, as said below
- spare_expert: int32 [32], P('groups'), parts along dimension 0, may hold values from -1 to 15, as said below
Outputs:
- moe_out: bfloat16 [2048, 2048], P(('groups', 'ep')), parts along dimension 0
There are 2 independent parts, one for each index of `groups`. A program takes and returns all parts, laid end to end along the dimension named above; each array names one. Nothing has to cross between parts.
Inputs may be any that keep to these rules, and one draw needn't show every extreme that they name: `expert_ids`: each row names 8 different experts. `home_slot`: a permutation of the experts. `spare_expert`: each expert is named a multiple of 3 times, at most 6, and some expert exactly 3 * 2 times; -1 stands in as many entries as the remainder of 16 divided by 3. `expert_weights`: the second slot of the device holding the k-th third of a split copy of expert e equals the matching gate, up and down columns (hidden units k * 256 to (k + 1) * 256 - 1) of e's home block.
All inputs are finite; a program needn't handle non-finite values.
Results may differ from a plain program's by a relative error of at most 0.0058.
Values may be sent and summed in bfloat16 or wider, within the bound.
A program may use at most 128 MiB of HBM per device.

v0:
```python
import jax
import jax.numpy as jnp
from jax import lax
from jax.sharding import PartitionSpec as P


def expert_rows(token_rows, weight_block):
    hidden_width = weight_block.shape[1] // 3
    gate_up = jnp.dot(
        token_rows, weight_block[:, : 2 * hidden_width], preferred_element_type=jnp.float32
    )
    hidden = (jax.nn.silu(gate_up[:, :hidden_width]) * gate_up[:, hidden_width:]).astype(
        jnp.bfloat16
    )
    answer = lax.dot_general(
        hidden,
        weight_block[:, 2 * hidden_width :],
        (((1,), (1,)), ((), ())),
        preferred_element_type=jnp.float32,
    )
    return answer.astype(jnp.bfloat16)


def third_rows(token_rows, third_block):
    third_width = third_block.shape[1] // 3
    gate_up = jnp.dot(
        token_rows, third_block[:, : 2 * third_width], preferred_element_type=jnp.float32
    )
    hidden = (jax.nn.silu(gate_up[:, :third_width]) * gate_up[:, third_width:]).astype(jnp.bfloat16)
    return lax.dot_general(
        hidden,
        third_block[:, 2 * third_width :],
        (((1,), (1,)), ((), ())),
        preferred_element_type=jnp.float32,
    )


def routing(expert_ids, home_slot, spare_expert):
    experts = home_slot.shape[0]
    flat_ids = expert_ids.reshape(-1)
    expert_range = jnp.arange(experts, dtype=jnp.int32)
    holders = (spare_expert[None, :] == expert_range[:, None]).astype(jnp.int32)
    copies = 1 + jnp.sum(holders, axis=1) // 3
    holder_rank = jnp.cumsum(holders, axis=1) * holders
    chosen = (flat_ids[:, None] == expert_range[None, :]).astype(jnp.int32)
    earlier = jnp.cumsum(chosen, axis=0) - chosen
    arrival = jnp.sum(earlier * chosen, axis=1)
    copy_count = jnp.sum(chosen * copies[None, :], axis=1)
    home_device = jnp.sum(chosen * home_slot[None, :], axis=1)
    copy_index = arrival % copy_count
    position = arrival // copy_count
    rank_rows = jnp.dot(chosen, holder_rank)
    return (home_device, copy_index, position, rank_rows)


def shards(tokens, expert_ids, gate_values, expert_weights, home_slot, spare_expert):
    devices = lax.axis_size("ep")
    local_tokens = tokens.shape[0]
    feature = tokens.shape[1]
    top_count = expert_ids.shape[1]
    capacity = local_tokens * top_count // devices
    hidden_width = expert_weights.shape[2] // 4
    home_block = expert_weights[0, :, : 3 * hidden_width]
    repeated = jnp.repeat(tokens, top_count, axis=0)
    home_device, copy_index, position, rank_rows = routing(expert_ids, home_slot, spare_expert)
    served = position < capacity
    gate_flat = gate_values.reshape(-1)
    spare_block = expert_weights[0, :, 3 * hidden_width :]
    overflow = devices * capacity
    first_copy = served & (copy_index == 0)
    split_copy = served & (copy_index > 0)
    device_range = jnp.arange(devices, dtype=jnp.int32)
    home_target = jnp.where(first_copy, home_device * capacity + position, overflow)
    home_box = (
        jnp.zeros((overflow, feature), jnp.bfloat16).at[home_target].set(repeated, mode="drop")
    )
    spare_box = jnp.zeros((overflow, feature), jnp.bfloat16)
    third_targets = []
    for third_index in range(3):
        wanted = 3 * copy_index - 2 + third_index
        holder = jnp.sum(jnp.where(rank_rows == wanted[:, None], device_range[None, :], 0), axis=1)
        third_target = jnp.where(split_copy, holder * capacity + position, overflow)
        spare_box = spare_box.at[third_target].set(repeated, mode="drop")
        third_targets.append(third_target)
    outbox = (
        home_box.reshape(devices, capacity, feature),
        spare_box.reshape(devices, capacity, feature),
    )
    home_rows = lax.all_to_all(outbox[0], "ep", split_axis=0, concat_axis=0, tiled=True)
    spare_rows = lax.all_to_all(outbox[1], "ep", split_axis=0, concat_axis=0, tiled=True)
    answers = expert_rows(home_rows.reshape(-1, feature), home_block).reshape(home_rows.shape)
    partials = third_rows(spare_rows.reshape(-1, feature), spare_block).reshape(spare_rows.shape)
    answers_back = lax.all_to_all(answers, "ep", split_axis=0, concat_axis=0, tiled=True)
    partials_back = lax.all_to_all(partials, "ep", split_axis=0, concat_axis=0, tiled=True)
    answers_back, partials_back = (answers_back, partials_back)
    home_values = jnp.take(
        answers_back.reshape(-1, feature), home_target, axis=0, mode="fill", fill_value=0
    ).astype(jnp.float32)
    flat_partials = partials_back.reshape(-1, feature)
    split_sum = jnp.zeros((home_target.shape[0], feature), jnp.float32)
    for third_target in third_targets:
        split_sum = split_sum + jnp.take(
            flat_partials, third_target, axis=0, mode="fill", fill_value=0
        )
    split_rounded = lax.optimization_barrier(split_sum.astype(jnp.bfloat16))
    split_values = split_rounded.astype(jnp.float32)
    values = jnp.where(first_copy[:, None], home_values, split_values)
    weighted = values * gate_flat[:, None]
    return jnp.sum(weighted.reshape(local_tokens, top_count, feature), axis=1).astype(jnp.bfloat16)


def solution(mesh):
    in_specs = (
        P(("groups", "ep"), None),
        P(("groups", "ep"), None),
        P(("groups", "ep"), None),
        P(("groups", "ep"), None, None),
        P("groups"),
        P("groups"),
    )
    out_specs = P(("groups", "ep"), None)
    return jax.shard_map(shards, mesh=mesh, in_specs=in_specs, out_specs=out_specs, check_vma=False)
```

profile of v0, /device:TPU:13, one launch (start us, length us, event | category | flops | bytes accessed | tf_op | source)
XLA Modules:
  0.0 297.1 jit_solution(1587522894917769411)
XLA Ops:
  0.0 0.0 copy-start
  0.0 0.8 copy.8
  0.8 0.1 eq.128
  0.9 0.1 eq.124
  1.0 1.2 reduce-window.6
  2.2 0.2 slice_reduce_fusion
  2.4 0.8 fusion.42
  3.2 0.8 select_reduce_fusion.3
  4.0 0.4 compare_select_fusion.3
  4.4 0.0 copy-done
  4.4 5.1 %scatter_custom_fusion = bf16[512,2048]{1,0:T(8,128)(2,1)} fusion(s32[512]{0:T(512)S(1)} %bitcast.60, bf16[64,2048]{1,0:T(8,128)(2,1)S(1)} %copy-done, bf16[]{:T(256)} %constant.73.clone.1), kind=kCustom, calls=%fused_computation.17 | custom fusion | bytes 2359298 | tf_op jit(solution)/shard_map/scatter | solution.py:75
  9.5 0.0 copy-start.4
  9.5 6.7 %all-to-all-start = ((bf16[16,32,2048]{2,1,0:T(8,128)(2,1)}), bf16[16,32,2048]{2,1,0:T(8,128)(2,1)S(1)}, u32[]{:S(2)}, u32[]{:S(2)}) async-start(bf16[16,32,2048]{2,1,0:T(8,128)(2,1)} %bitcast.6), calls=%async_computation | async-start | bytes 4194304 | tf_op jit(solution)/shard_map/all_to_all | solution.py:89
  16.2 0.0 copy-done.4
  16.2 0.2 reduce_window_sum.28
  16.4 0.1 compare_and_fusion.5
  16.5 0.2 select_reduce_fusion
  16.8 5.1 %scatter_custom_fusion.1 = bf16[512,2048]{1,0:T(8,128)(2,1)} fusion(s32[512]{0:T(512)S(1)} %bitcast.68, bf16[64,2048]{1,0:T(8,128)(2,1)S(1)} %copy-done, bf16[]{:T(256)} %constant.73.clone.1), kind=kCustom, calls=%fused_computation.15 | custom fusion | bytes 2359298 | tf_op jit(solution)/shard_map/scatter | solution.py:83
  21.9 6.7 %scatter_custom_fusion.2 = bf16[512,2048]{1,0:T(8,128)(2,1)} fusion(bf16[512,2048]{1,0:T(8,128)(2,1)} %scatter_custom_fusion.1, s32[512]{0:T(512)S(1)} %bitcast.67, bf16[64,2048]{1,0:T(8,128)(2,1)S(1)} %copy-done), kind=kCustom, calls=%fused_computation.13 | custom fusion | bytes 2359296 | tf_op jit(solution)/shard_map/scatter | solution.py:83
  28.6 6.7 %scatter_custom_fusion.3 = bf16[512,2048]{1,0:T(8,128)(2,1)} fusion(bf16[512,2048]{1,0:T(8,128)(2,1)} %scatter_custom_fusion.2, s32[512]{0:T(512)S(1)} %bitcast.66, bf16[64,2048]{1,0:T(8,128)(2,1)S(1)} %copy-done), kind=kCustom, calls=%fused_computation.11 | custom fusion | bytes 2359296 | tf_op jit(solution)/shard_map/scatter | solution.py:83
  35.2 28.4 %all-to-all-done = bf16[16,32,2048]{2,1,0:T(8,128)(2,1)S(1)} async-done(((bf16[16,32,2048]{2,1,0:T(8,128)(2,1)}), bf16[16,32,2048]{2,1,0:T(8,128)(2,1)S(1)}, u32[]{:S(2)}, u32[]{:S(2)}) %all-to-all-start) | async-done | bytes 2097184 | tf_op jit(solution)/shard_map/all_to_all | solution.py:89
  63.6 4.9 %all-to-all-start.2 = ((bf16[16,32,2048]{2,1,0:T(8,128)(2,1)}), bf16[16,32,2048]{2,1,0:T(8,128)(2,1)}, u32[]{:S(2)}, u32[]{:S(2)}) async-start(bf16[16,32,2048]{2,1,0:T(8,128)(2,1)} %bitcast.17), calls=%async_computation.2 | async-start | bytes 4194304 | tf_op jit(solution)/shard_map/all_to_all | solution.py:90
  68.5 7.9 %slice_bitcast_fusion = bf16[2048,2304]{1,0:T(8,128)(2,1)} fusion(bf16[1,2048,3072]{2,1,0:T(8,128)(2,1)} %param.11), kind=kLoop, calls=%fused_computation.8 | loop fusion | bytes 18874368 | tf_op jit(solution)/shard_map/squeeze | solution.py:63
  76.4 5.5 %fusion = f32[512,1536]{1,0:T(8,128)S(1)} fusion(bf16[512,2048]{1,0:T(8,128)(2,1)S(1)} %bitcast.56, bf16[2048,2304]{1,0:T(8,128)(2,1)} %slice_bitcast_fusion), kind=kOutput, calls=%fused_computation.9 | convolution fusion | flops 3221225472 | bytes 11534336 | tf_op jit(solution)/shard_map/dot_general | solution.py:9
  81.9 5.2 %fusion.13 = bf16[512,2048]{1,0:T(8,128)(2,1)} fusion(bf16[2048,2304]{1,0:T(8,128)(2,1)} %slice_bitcast_fusion, f32[512,1536]{1,0:T(8,128)S(1)} %fusion), kind=kOutput, calls=%fused_computation.26 | convolution fusion | flops 1614020608 | bytes 8388608 | tf_op jit(solution)/shard_map/dot_general | solution.py:15
  87.1 28.9 %all-to-all-done.2 = bf16[16,32,2048]{2,1,0:T(8,128)(2,1)} async-done(((bf16[16,32,2048]{2,1,0:T(8,128)(2,1)}), bf16[16,32,2048]{2,1,0:T(8,128)(2,1)}, u32[]{:S(2)}, u32[]{:S(2)}) %all-to-all-start.2) | async-done | bytes 2097184 | tf_op jit(solution)/shard_map/all_to_all | solution.py:90
  116.0 4.9 %all-to-all-start.1 = ((bf16[16,32,2048]{2,1,0:T(8,128)(2,1)}), bf16[16,32,2048]{2,1,0:T(8,128)(2,1)S(1)}, u32[]{:S(2)}, u32[]{:S(2)}) async-start(bf16[16,32,2048]{2,1,0:T(8,128)(2,1)} %bitcast.57), calls=%async_computation.1 | async-start | bytes 4194304 | tf_op jit(solution)/shard_map/all_to_all | solution.py:93
  121.0 2.1 slice_bitcast_fusion.1
  123.1 2.8 fusion.16
  125.9 2.7 fusion.19
  128.6 39.8 %all-to-all-done.1 = bf16[16,32,2048]{2,1,0:T(8,128)(2,1)S(1)} async-done(((bf16[16,32,2048]{2,1,0:T(8,128)(2,1)}), bf16[16,32,2048]{2,1,0:T(8,128)(2,1)S(1)}, u32[]{:S(2)}, u32[]{:S(2)}) %all-to-all-start.1) | async-done | bytes 2097184 | tf_op jit(solution)/shard_map/all_to_all | solution.py:93
  168.4 0.0 copy-start.3
  168.4 5.0 %all-to-all-start.3 = ((f32[16,32,2048]{2,1,0:T(8,128)}), f32[16,32,2048]{2,1,0:T(8,128)}, u32[]{:S(2)}, u32[]{:S(2)}) async-start(f32[16,32,2048]{2,1,0:T(8,128)} %bitcast.55), calls=%async_computation.3 | async-start | bytes 8388608 | tf_op jit(solution)/shard_map/all_to_all | solution.py:94
  173.4 0.0 copy-done.3
  173.4 0.1 copy.11
  173.5 0.1 mul.134
  173.7 3.3 %gather_fusion = bf16[512,2048]{1,0:T(8,128)(2,1)} fusion(bf16[512,2048]{1,0:T(8,128)(2,1)S(1)} %bitcast.54, s32[1024]{0:T(1024)S(1)} %pad_clamp_fusion.3), kind=kCustom, calls=%fused_computation.3 | custom fusion | bytes 4196352 | tf_op jit(solution)/shard_map/jit(_take)/gather | solution.py:96
  177.0 88.9 %all-to-all-done.3 = f32[16,32,2048]{2,1,0:T(8,128)} async-done(((f32[16,32,2048]{2,1,0:T(8,128)}), f32[16,32,2048]{2,1,0:T(8,128)}, u32[]{:S(2)}, u32[]{:S(2)}) %all-to-all-start.3) | async-done | bytes 4194336 | tf_op jit(solution)/shard_map/all_to_all | solution.py:94
  265.9 7.6 %gather_fusion.1 = f32[512,2048]{1,0:T(8,128)} fusion(f32[512,2048]{1,0:T(8,128)} %bitcast.21, s32[1024]{0:T(1024)S(1)} %pad_clamp_fusion.2), kind=kCustom, calls=%fused_computation.clone | custom fusion | bytes 8390656 | tf_op jit(solution)/shard_map/jit(_take)/gather | solution.py:102
  273.5 7.6 %gather_fusion.2 = f32[512,2048]{1,0:T(8,128)} fusion(f32[512,2048]{1,0:T(8,128)} %bitcast.21, s32[1024]{0:T(1024)S(1)} %get-tuple-element.38), kind=kCustom, calls=%fused_computation.1.clone | custom fusion | bytes 8390656 | tf_op jit(solution)/shard_map/jit(_take)/gather | solution.py:102
  281.1 7.6 %gather_fusion.3 = f32[512,2048]{1,0:T(8,128)} fusion(f32[512,2048]{1,0:T(8,128)} %bitcast.21, s32[1024]{0:T(1024)S(1)} %get-tuple-element.37), kind=kCustom, calls=%fused_computation.2.clone | custom fusion | bytes 8390656 | tf_op jit(solution)/shard_map/jit(_take)/gather | solution.py:102
  288.7 0.0 copy-start.2
  288.7 5.4 %fusion.10 = bf16[512,2048]{1,0:T(8,128)(2,1)S(1)} fusion(f32[512,2048]{1,0:T(8,128)} %gather_fusion.3, f32[512,2048]{1,0:T(8,128)} %gather_fusion.2, f32[512,2048]{1,0:T(8,128)} %gather_fusion.1, pred[512]{0:T(512)(128)(4,1)S(1)} %get-tuple-element.30, pred[512]{0:T(512)(128)(4,1)S(1)} %get-tuple-element.23, pred[512]{0:T(512)(128)(4,1)S(1)} %get-tuple-element.20), kind=kLoop, calls=%fused_computation.21 | loop fusion | flops 6291456 | bytes 14681600 | tf_op jit(solution)/shard_map/convert_element_type | solution.py:105
  294.0 0.0 copy-start.1
  294.0 0.0 copy-done.2
  294.1 3.0 %bitcast_reduce_fusion = bf16[64,2048]{1,0:T(8,128)(2,1)} fusion(bf16[512,2048]{1,0:T(8,128)(2,1)S(1)} %fusion.10, f32[512]{0:T(512)S(1)} %mul.134, bf16[512,2048]{1,0:T(8,128)(2,1)S(1)} %copy-done.2, pred[512]{0:T(512)(128)(4,1)S(1)} %get-tuple-element.12, pred[512]{0:T(512)(128)(4,1)S(1)} %get-tuple-element.13), kind=kLoop, calls=%fused_computation.19 | loop fusion | flops 6160384 | bytes 4459520 | tf_op jit(solution)/shard_map/reduce_sum | solution.py:109
  297.1 0.0 copy-done.1
  (15 shorter events, 0.1 us)
Async XLA Ops:
  0.0 4.4 %copy-start = (bf16[64,2048]{1,0:T(8,128)(2,1)S(1)}, bf16[64,2048]{1,0:T(8,128)(2,1)}, u32[]{:S(2)}) copy-start(bf16[64,2048]{1,0:T(8,128)(2,1)} %param.8) | copy-start | bytes 786436
  9.5 6.7 %copy-start.4 = (s32[16]{0:T(128)S(1)}, s32[16]{0:T(128)}, u32[]{:S(2)}) copy-start(s32[16]{0:T(128)} %param.13) | copy-start | bytes 196
  9.5 54.1 %all-to-all-start = ((bf16[16,32,2048]{2,1,0:T(8,128)(2,1)}), bf16[16,32,2048]{2,1,0:T(8,128)(2,1)S(1)}, u32[]{:S(2)}, u32[]{:S(2)}) async-start(bf16[16,32,2048]{2,1,0:T(8,128)(2,1)} %bitcast.6), calls=%async_computation | async-start | bytes 4194304 | tf_op jit(solution)/shard_map/all_to_all | solution.py:89
  63.6 52.4 %all-to-all-start.2 = ((bf16[16,32,2048]{2,1,0:T(8,128)(2,1)}), bf16[16,32,2048]{2,1,0:T(8,128)(2,1)}, u32[]{:S(2)}, u32[]{:S(2)}) async-start(bf16[16,32,2048]{2,1,0:T(8,128)(2,1)} %bitcast.17), calls=%async_computation.2 | async-start | bytes 4194304 | tf_op jit(solution)/shard_map/all_to_all | solution.py:90
  116.0 52.3 %all-to-all-start.1 = ((bf16[16,32,2048]{2,1,0:T(8,128)(2,1)}), bf16[16,32,2048]{2,1,0:T(8,128)(2,1)S(1)}, u32[]{:S(2)}, u32[]{:S(2)}) async-start(bf16[16,32,2048]{2,1,0:T(8,128)(2,1)} %bitcast.57), calls=%async_computation.1 | async-start | bytes 4194304 | tf_op jit(solution)/shard_map/all_to_all | solution.py:93
  168.4 5.0 %copy-start.3 = (f32[64,8]{0,1:T(8,128)S(1)}, f32[64,8]{0,1:T(8,128)}, u32[]{:S(2)}) copy-start(f32[64,8]{0,1:T(8,128)} %param.10) | copy-start | bytes 6148
  168.4 97.5 %all-to-all-start.3 = ((f32[16,32,2048]{2,1,0:T(8,128)}), f32[16,32,2048]{2,1,0:T(8,128)}, u32[]{:S(2)}, u32[]{:S(2)}) async-start(f32[16,32,2048]{2,1,0:T(8,128)} %bitcast.55), calls=%async_computation.3 | async-start | bytes 8388608 | tf_op jit(solution)/shard_map/all_to_all | solution.py:94
  288.7 5.4 %copy-start.2 = (bf16[512,2048]{1,0:T(8,128)(2,1)S(1)}, bf16[512,2048]{1,0:T(8,128)(2,1)}, u32[]{:S(2)}) copy-start(bf16[512,2048]{1,0:T(8,128)(2,1)} %gather_fusion) | copy-start | bytes 6291460
  294.0 3.1 %copy-start.1 = (bf16[64,2048]{1,0:T(8,128)(2,1)S(1)}, bf16[64,2048]{1,0:T(8,128)(2,1)}, u32[]{:S(2)}) copy-start(bf16[64,2048]{1,0:T(8,128)(2,1)} %param.8) | copy-start | bytes 786436
where the time goes:
time: 298 us; the launch traced here: 297 us
  waiting for transfers between devices  186 us (62%)
  local copies, waits for them, and re-layouts  61.1 us (21%)
  starting transfers between devices  21.5 us (7%)
  matrix products  16.5 us (6%)
  other arithmetic  11.9 us (4%)
    all_to_all x1, waiting for transfers between devices, shards(): lax.all_to_all(partials, 'ep', split_axis=0, concat_axis=0, tiled=True)  88.9 us
    all_to_all x1, waiting for transfers between devices, shards(): lax.all_to_all(answers, 'ep', split_axis=0, concat_axis=0, tiled=True)  39.8 us
    all_to_all x1, waiting for transfers between devices, shards(): lax.all_to_all(outbox[1], 'ep', split_axis=0, concat_axis=0, tiled=True)  28.9 us
    all_to_all x1, waiting for transfers between devices, shards(): lax.all_to_all(outbox[0], 'ep', split_axis=0, concat_axis=0, tiled=True)  28.4 us
    gather x3, local copies, waits for them, and re-layouts, shards(): jnp.take(flat_partials, third_target, axis=0, mode='fill', fill_value=0)  22.8 us
    scatter x3, local copies, waits for them, and re-layouts, shards(): spare_box = spare_box.at[third_target].set(repeated, mode='drop')  18.4 us
    squeeze x1, local copies, waits for them, and re-layouts, shards(): home_block = expert_weights[0, :, :3 * hidden_width]  7.91 us
    all_to_all x1, starting transfers between devices, shards(): lax.all_to_all(outbox[0], 'ep', split_axis=0, concat_axis=0, tiled=True)  6.69 us
  transfers between devices with their start and end apart: 4, of which 4 were waited for; matrix products, arithmetic and copies ran while one was open for 16% of the time, Pallas kernels for 0%

commit v1 on v0

v1 whole, which is shorter than its diff:
```python
import jax
import jax.numpy as jnp
from jax import lax
from jax.sharding import PartitionSpec as P


def device_gates(expert_ids, gate_values, home_slot, spare_expert, capacity):
    count = home_slot.shape[0]
    span = jnp.arange(count, dtype=jnp.int32)
    expert_of = jnp.sum(jnp.where(home_slot[None, :] == span[:, None], span[None, :], 0), axis=1)
    thirds = jnp.sum((spare_expert[None, :] == expert_of[:, None]).astype(jnp.int32), axis=1)
    limit = capacity * (1 + thirds // 3)
    match = expert_ids[:, :, None] == expert_of[None, None, :]
    gates = jnp.sum(jnp.where(match, gate_values[:, :, None], 0.0), axis=1)
    named = jnp.any(match, axis=1)
    rows = jnp.arange(expert_ids.shape[0], dtype=jnp.int32)
    before = (rows[None, :] < rows[:, None]).astype(jnp.bfloat16)
    arrival = jnp.dot(before, named.astype(jnp.bfloat16), preferred_element_type=jnp.float32)
    return jnp.where(named & (arrival < limit[None, :].astype(jnp.float32)), gates, 0.0)


def shards(tokens, expert_ids, gate_values, expert_weights, home_slot, spare_expert):
    devices = lax.axis_size("ep")
    me = lax.axis_index("ep")
    local_tokens, feature = tokens.shape
    capacity = local_tokens * expert_ids.shape[1] // devices
    width = expert_weights.shape[2] // 4
    block = expert_weights[0, :, : 3 * width]
    gates = device_gates(expert_ids, gate_values, home_slot, spare_expert, capacity)
    everything = lax.all_gather(tokens, "ep", axis=0, tiled=True)
    gates_all = lax.all_gather(gates, "ep", axis=0, tiled=True)
    mine = lax.dynamic_slice_in_dim(gates_all, me, 1, axis=1)
    gate_up = jnp.dot(everything, block[:, : 2 * width], preferred_element_type=jnp.float32)
    hidden = (jax.nn.silu(gate_up[:, :width]) * gate_up[:, width:]).astype(jnp.bfloat16)
    answer = lax.dot_general(
        hidden, block[:, 2 * width :], (((1,), (1,)), ((), ())), preferred_element_type=jnp.float32
    )
    weighted = jnp.where(mine > 0, answer * mine, 0.0).astype(jnp.bfloat16)
    return lax.psum_scatter(weighted, "ep", scatter_dimension=0, tiled=True).astype(jnp.bfloat16)


def solution(mesh):
    in_specs = (
        P(("groups", "ep"), None),
        P(("groups", "ep"), None),
        P(("groups", "ep"), None),
        P(("groups", "ep"), None, None),
        P("groups"),
        P("groups"),
    )
    out_specs = P(("groups", "ep"), None)
    return jax.shard_map(shards, mesh=mesh, in_specs=in_specs, out_specs=out_specs, check_vma=False)
```

time: 298 us -> 159 us (0.53)
  the two profiles are of different devices: /device:TPU:13 before, /device:TPU:0 now
where the time goes in v1:
time: 159 us
  waiting for transfers between devices  92.8 us (58%)
  blocking collectives  23.7 us (15%)
  matrix products  17.4 us (11%)
  between operations  13.4 us (8%)
  local copies, waits for them, and re-layouts  8.05 us (5%)
  other arithmetic  3.21 us (2%)
    reduce_scatter x1, waiting for transfers between devices, shards(): lax.psum_scatter(weighted, 'ep', scatter_dimension=0, tiled=True)  71.3 us
    all_gather x1, blocking collectives, shards(): gates_all = lax.all_gather(gates, 'ep', axis=0, tiled=True)  23.7 us
    all_gather x1, waiting for transfers between devices, shards(): everything = lax.all_gather(tokens, 'ep', axis=0, tiled=True)  20.7 us
    dot_general x1, matrix products, shards(): jnp.dot(everything, block[:, :2 * width], preferred_element_type=jnp.floa...  10 us
    squeeze x1, local copies, waits for them, and re-layouts, shards(): block = expert_weights[0, :, :3 * width]  7.91 us
    dot_general x1, matrix products, shards(): lax.dot_general(hidden, block[:, 2 * width:], (((1,), (1,)), ((), ())), p...  7.25 us
  transfers between devices with their start and end apart: 2, of which 2 were waited for; matrix products, arithmetic and copies ran while one was open for 7% of the time, Pallas kernels for 0%

profile of v1, /device:TPU:0, one launch (start us, length us, event | category | flops | bytes accessed | tf_op | source)
XLA Modules:
  0.0 158.6 jit_solution(4060753552183969313)
XLA Ops:
  6.5 0.0 all-gather.3.cloned.1.call-start
  6.5 0.7 all-gather.3.cloned.1.call-update
  7.3 0.0 reduce-scatter.2.cloned.1.call-start
  7.3 0.8 select_reduce_fusion
  8.1 0.8 convert_reduce_fusion
  8.9 0.8 compare_reduce_fusion
  9.7 0.8 fusion.9
  10.5 0.1 fusion.8
  10.6 23.7 %all-gather = f32[16,64,16]{1,2,0:T(8,128)S(1)} all-gather(f32[1,64,16]{1,2,0:T(8,128)S(1)} %fusion.8), channel_id=1, replica_groups=mesh['groups'=2,'ep'=16] {'ep'}, dimensions={0}, use_global_device_ids=true | all-gather | bytes 69632 | tf_op jit(solution)/shard_map/all_gather | solution.py:31
  34.4 0.1 reshape.21
  34.5 7.9 %slice_bitcast_fusion = bf16[2048,2304]{1,0:T(8,128)(2,1)} fusion(bf16[1,2048,3072]{2,1,0:T(8,128)(2,1)} %param.9), kind=kLoop, calls=%fused_computation | loop fusion | bytes 18874368 | tf_op jit(solution)/shard_map/squeeze | solution.py:28
  42.4 20.7 %all-gather.3.cloned.1.call-done = bf16[1024,2048]{1,0:T(8,128)(2,1)} async-done(((bf16[64,2048]{1,0:T(8,128)(2,1)}), bf16[1024,2048]{1,0:T(8,128)(2,1)}) %all-gather.3.cloned.1.call-update) | async-done | bytes 4194320 | tf_op jit(solution)/shard_map/all_gather | solution.py:30
  63.1 10.0 %fusion = f32[1024,1536]{1,0:T(8,128)S(1)} fusion(bf16[1024,2048]{1,0:T(8,128)(2,1)} %all-gather.3.cloned.1.call-done, bf16[2048,2304]{1,0:T(8,128)(2,1)} %slice_bitcast_fusion), kind=kOutput, calls=%fused_computation.2 | convolution fusion | flops 6442450944 | bytes 16777216 | tf_op jit(solution)/shard_map/dot_general | solution.py:33
  73.2 7.3 %select_convert_fusion = bf16[1024,2048]{1,0:T(8,128)(2,1)} fusion(f32[1024]{0:T(1024)S(1)} %bitcast.9, pred[1024]{0:T(1024)(128)(4,1)S(1)} %get-tuple-element.5, bf16[2048,2304]{1,0:T(8,128)(2,1)} %slice_bitcast_fusion, f32[1024,1536]{1,0:T(8,128)S(1)} %fusion), kind=kOutput, calls=%fused_computation.1 | convolution fusion | flops 3232235520 | bytes 13636608 | tf_op jit(solution)/shard_map/dot_general | solution.py:35
  80.4 0.0 reduce-scatter.2.cloned.1.call-update
  80.4 71.3 %reduce-scatter.2.cloned.1.call-done = bf16[64,2048]{1,0:T(8,128)(2,1)} async-done(((bf16[1024,2048]{1,0:T(8,128)(2,1)}), bf16[64,2048]{1,0:T(8,128)(2,1)}) %reduce-scatter.2.cloned.1.call-update) | async-done | bytes 262160 | tf_op jit(solution)/shard_map/reduce_scatter | solution.py:39
  (3 shorter events, 0.1 us)
Async XLA Ops:
  6.5 56.6 %all-gather.3.cloned.1.call-start = ((), (), s32[]{:S(2)}) async-start(), calls=%async_computation.1 | async-start | bytes 4456448 | tf_op jit(solution)/shard_map/all_gather | solution.py:30
  7.3 144.5 %reduce-scatter.2.cloned.1.call-start = ((), (), s32[]{:S(2)}) async-start(), calls=%async_computation.2 | async-start | bytes 4456448 | tf_op jit(solution)/shard_map/reduce_scatter | solution.py:39
Sparse Core Ops, SparseCore 0:
  9.5 53.5 all-gather.2
  80.6 71.1 reduce-scatter.1

commit v2 on v1

--- a/solution.py
+++ b/solution.py
@@ -1,6 +1,10 @@
+import functools
+
 import jax
 import jax.numpy as jnp
 from jax import lax
+from jax.experimental import pallas as pl
+from jax.experimental.pallas import tpu as pltpu
 from jax.sharding import PartitionSpec as P
 
 
@@ -19,24 +23,263 @@
     return jnp.where(named & (arrival < limit[None, :].astype(jnp.float32)), gates, 0.0)
 
 
+MESH = pl.DeviceIdType.MESH
+
+
+def fused(devices, feature, width, x_ref, w_hbm, out_ref, xall, w, hid, part, sib_out, sib_in, rs,
+          w_sem, ag_send, ag_recv, sx_send, sx_recv, sr_send, sr_recv, rs_send, rs_recv):
+    chips = devices // 2
+    far = chips // 2
+    me = lax.axis_index("ep")
+    core = me % 2
+    chip = me // 2
+    odd = chip % 2
+    place = (1 - odd) * (chip // 2) + odd * (chips - 1 - chip // 2)
+
+    def device_at(spot):
+        low = 1 - spot // far
+        return 2 * (low * 2 * spot + (1 - low) * (2 * (chips - 1 - spot) + 1)) + core
+
+    right = device_at((place + 1) % chips)
+    left = device_at((place + chips - 1) % chips)
+    sibling = me + 1 - 2 * core
+    toward = (right, left)
+
+    def remote(src, dst, send, recv, device):
+        return pltpu.make_async_remote_copy(src_ref=src, dst_ref=dst, send_sem=send, recv_sem=recv,
+                                            device_id={"ep": device}, device_id_type=MESH)
+
+    def gather(side, d, half):
+        src_side = 0 if isinstance(d, int) and d == 0 else side
+        dst_side = 0 if side == 0 else 1 - (d + 1) // far
+        return remote(xall.at[d, src_side, core, half], xall.at[d + 1, dst_side, core, half],
+                      ag_send.at[side, d, half], ag_recv.at[side, d + 1, half], toward[side])
+
+    def share(side, d, half):
+        slot = xall.at[d, side, core, half]
+        return remote(slot, slot, sx_send.at[side, d, half], sx_recv.at[side, d, half], sibling)
+
+    def exchange(slot, side, d):
+        return remote(sib_out.at[slot, side], sib_in.at[d, side],
+                      sr_send.at[slot, side], sr_recv.at[d, side], sibling)
+
+    def reduce(way, d, half):
+        return remote(rs.at[way, d, half], rs.at[way, d - 1, half],
+                      rs_send.at[way, d, half], rs_recv.at[way, d - 1, half], toward[1 - way])
+
+    def up(d, sides):
+        rows = sides * 2 * x_ref.shape[0] * x_ref.shape[1]
+        tile = 256
+
+        @pl.loop(0, width // tile)
+        def _(f):
+            x = xall[d, :sides, :, :, :, :feature].reshape(rows, feature)
+            at = pl.multiple_of(f * tile, tile)
+            gate = jnp.dot(x, w[:, pl.ds(at, tile)], preferred_element_type=jnp.float32)
+            lift = jnp.dot(x, w[:, pl.ds(width + at, tile)], preferred_element_type=jnp.float32)
+            hid[:rows, pl.ds(at, tile)] = (gate * lax.logistic(gate) * lift).astype(jnp.bfloat16)
+
+    def down(d, sides, slot):
+        half_rows = x_ref.shape[1]
+        rows = sides * 4 * half_rows
+        extra = xall[d, :sides, :, :, :, feature:].reshape(rows, -1).astype(jnp.float32)
+        lane = lax.broadcasted_iota(jnp.int32, extra.shape, 1)
+        gates = jnp.sum(jnp.where((lane == me) | (lane == me + devices), extra, 0.0), axis=1, keepdims=True)
+        tile = 512
+
+        @pl.loop(0, feature // tile)
+        def _(o):
+            at = pl.multiple_of(o * tile, tile)
+            answer = lax.dot_general(hid[:rows], w[pl.ds(at, tile), 2 * width:],
+                                     (((1,), (1,)), ((), ())), preferred_element_type=jnp.float32)
+            answer = answer.astype(jnp.bfloat16).astype(jnp.float32)
+            value = jnp.where(gates > 0, answer * gates, 0.0).reshape(sides, 2, 2, half_rows, tile)
+            mine = jnp.where(core == 0, value[:, 0], value[:, 1])
+            other = jnp.where(core == 0, value[:, 1], value[:, 0])
+            part[d, :sides, :, :, pl.ds(at, tile)] = mine.astype(part.dtype)
+            sib_out[slot, :sides, :, :, pl.ds(at, tile)] = other.astype(jnp.bfloat16)
+
+        for side in range(sides):
+            exchange(slot, side, d).start()
+
+    def total(side, d, half):
+        return part[d, side, half].astype(jnp.float32) + sib_in[d, side, half].astype(jnp.float32)
+
+    def pass_on(way, d, half):
+        reduce(way, d + 1, half).wait_recv()
+        rs[way, d, half] = (total(way, d, half) + rs[way, d, half].astype(jnp.float32)).astype(jnp.bfloat16)
+        reduce(way, d, half).start()
+
+    weights = pltpu.make_async_copy(w_hbm.at[0, :, pl.ds(0, 3 * width)], w, w_sem)
+    weights.start()
+    xall[0, 0, core] = x_ref[...]
+    barrier = pltpu.get_barrier_semaphore()
+    for device in (right, left, sibling):
+        pl.semaphore_signal(barrier, inc=1, device_id={"ep": device}, device_id_type=MESH)
+    pl.semaphore_wait(barrier, 3)
+
+    for turn in range(2):
+        for side in range(2):
+            gather(side, 0, turn if side == 0 else 1 - turn).start()
+        share(0, 0, turn).start()
+    for half in range(2):
+        share(0, 0, half).wait_recv()
+    weights.wait()
+    up(0, 1)
+    for side in range(2):
+        gather(side, 0, side).wait_recv()
+        gather(side, 1, side).start()
+        share(side, 1, side).start()
+    down(0, 1, 2)
+    for side in range(2):
+        gather(side, 0, 1 - side).wait_recv()
+        gather(side, 1, 1 - side).start()
+        share(side, 1, 1 - side).start()
+
+    @pl.loop(2, far + 1)
+    def _(d):
+        last = d // far
+        for side in range(2):
+            gather(side, d - 1, side).wait_recv()
+
+        @pl.when(last == 0)
+        def _():
+            for side in range(2):
+                gather(side, d, side).start()
+                share(side, d, side).start()
+
+        @pl.when(last == 1)
+        def _():
+            for half in range(2):
+                share(0, far, half).start()
+
+        for side in range(2):
+            for half in range(2):
+                share(side, d - 1, half).wait_recv()
+        up(d - 1, 2)
+
+        @pl.when(last == 0)
+        def _():
+            for side in range(2):
+                gather(side, d - 1, 1 - side).wait_recv()
+
+                @pl.when(d < far - 1)
+                def _():
+                    gather(side, d, 1 - side).start()
+                share(side, d, 1 - side).start()
+
+        @pl.when(d >= 4)
+        def _():
+            for side in range(2):
+                exchange((d - 1) % 2, side, d - 3).wait_send()
+        down(d - 1, 2, (d - 1) % 2)
+
+    for half in range(2):
+        share(0, far, half).wait_recv()
+    up(far, 1)
+    for side in range(2):
+        exchange((far - 1) % 2, side, far - 1).wait_recv()
+    for way in range(2):
+        half = way
+        rs[way, far - 1, half] = total(way, far - 1, half).astype(jnp.bfloat16)
+        reduce(way, far - 1, half).start()
+    down(far, 1, 3)
+    exchange(3, 0, far).wait_recv()
+    for way in range(2):
+        half = 1 - way
+        rs[way, far, half] = total(0, far, half).astype(jnp.bfloat16)
+        reduce(way, far, half).start()
+
+    @pl.loop(1, far - 1)
+    def _(back):
+        d = far - back
+        for side in range(2):
+            exchange(0, side, d - 1).wait_recv()
+        for way in range(2):
+            pass_on(way, d - 1, way)
+        for way in range(2):
+            pass_on(way, d, 1 - way)
+
+    for way in range(2):
+        pass_on(way, 1, 1 - way)
+    exchange(2, 0, 0).wait_recv()
+    for half in range(2):
+        for way in range(2):
+            reduce(way, 1, half).wait_recv()
+        out_ref[half] = (total(0, 0, half) + rs[0, 0, half].astype(jnp.float32)
+                         + rs[1, 0, half].astype(jnp.float32)).astype(out_ref.dtype)
+
+    for half in range(2):
+        share(0, 0, half).wait_send()
+        share(0, far, half).wait_send()
+        for side in range(2):
+            gather(side, 0, half).wait_send()
+    for side in range(2):
+        gather(side, far - 1, side).wait_send()
+        share(side, far - 1, 0).wait_send()
+        share(side, far - 1, 1).wait_send()
+        exchange((far - 1) % 2, side, far - 1).wait_send()
+        exchange((far - 2) % 2, side, far - 2).wait_send()
+        reduce(side, far, 1 - side).wait_send()
+    exchange(2, 0, 0).wait_send()
+    exchange(3, 0, far).wait_send()
+
+    @pl.loop(1, far - 1)
+    def _(d):
+        for side in range(2):
+            for half in range(2):
+                gather(side, d, half).wait_send()
+                share(side, d, half).wait_send()
+
+    @pl.loop(1, far)
+    def _(d):
+        for way in range(2):
+            for half in range(2):
+                reduce(way, d, half).wait_send()
+
+
 def shards(tokens, expert_ids, gate_values, expert_weights, home_slot, spare_expert):
     devices = lax.axis_size("ep")
-    me = lax.axis_index("ep")
     local_tokens, feature = tokens.shape
     capacity = local_tokens * expert_ids.shape[1] // devices
     width = expert_weights.shape[2] // 4
-    block = expert_weights[0, :, : 3 * width]
     gates = device_gates(expert_ids, gate_values, home_slot, spare_expert, capacity)
-    everything = lax.all_gather(tokens, "ep", axis=0, tiled=True)
-    gates_all = lax.all_gather(gates, "ep", axis=0, tiled=True)
-    mine = lax.dynamic_slice_in_dim(gates_all, me, 1, axis=1)
-    gate_up = jnp.dot(everything, block[:, : 2 * width], preferred_element_type=jnp.float32)
-    hidden = (jax.nn.silu(gate_up[:, :width]) * gate_up[:, width:]).astype(jnp.bfloat16)
-    answer = lax.dot_general(
-        hidden, block[:, 2 * width :], (((1,), (1,)), ((), ())), preferred_element_type=jnp.float32
-    )
-    weighted = jnp.where(mine > 0, answer * mine, 0.0).astype(jnp.bfloat16)
-    return lax.psum_scatter(weighted, "ep", scatter_dimension=0, tiled=True).astype(jnp.bfloat16)
+    high = lax.reduce_precision(gates, 8, 7)
+    extra = jnp.concatenate([high, gates - high], axis=1).astype(jnp.bfloat16)
+    extra = jnp.pad(extra, ((0, 0), (0, -extra.shape[1] % 128)))
+    half_rows = local_tokens // 2
+    x = jnp.concatenate([tokens, extra], axis=1).reshape(2, half_rows, -1)
+    far = devices // 4
+    kept = jnp.float32 if devices <= 16 else jnp.bfloat16
+    dma = pltpu.SemaphoreType.DMA
+    result = pl.pallas_call(
+        functools.partial(fused, devices, feature, width),
+        out_shape=jax.ShapeDtypeStruct((2, half_rows, feature), jnp.bfloat16),
+        in_specs=[pl.BlockSpec(memory_space=pltpu.VMEM), pl.BlockSpec(memory_space=pl.ANY)],
+        out_specs=pl.BlockSpec(memory_space=pltpu.VMEM),
+        scratch_shapes=[
+            pltpu.VMEM((far + 1, 2, 2) + x.shape, jnp.bfloat16),
+            pltpu.VMEM((feature, 3 * width), jnp.bfloat16),
+            pltpu.VMEM((4 * local_tokens, width), jnp.bfloat16),
+            pltpu.VMEM((far + 1, 2, 2, half_rows, feature), kept),
+            pltpu.VMEM((4, 2, 2, half_rows, feature), jnp.bfloat16),
+            pltpu.VMEM((far + 1, 2, 2, half_rows, feature), jnp.bfloat16),
+            pltpu.VMEM((2, far + 1, 2, half_rows, feature), jnp.bfloat16),
+            dma,
+            dma((2, far + 1, 2)),
+            dma((2, far + 1, 2)),
+            dma((2, far + 1, 2)),
+            dma((2, far + 1, 2)),
+            dma((4, 2)),
+            dma((far + 1, 2)),
+            dma((2, far + 1, 2)),
+            dma((2, far + 1, 2)),
+        ],
+        compiler_params=pltpu.CompilerParams(
+            collective_id=0, has_side_effects=True, vmem_limit_bytes=(44 if devices <= 16 else 62) * 2**20
+        ),
+    )(x, expert_weights)
+    return result.reshape(local_tokens, feature)
 
 
 def solution(mesh):

time: 159 us -> 63 us (0.40)
  waiting for transfers between devices: 92.8 us -> 0 us
  Pallas kernels: 0 us -> 57.6 us
  blocking collectives: 23.7 us -> 0 us
  matrix products: 17.4 us -> 0.09 us
  between operations: 13.4 us -> 0.03 us
  local copies, waits for them, and re-layouts: 8.05 us -> 0.8 us
    reduce_scatter x1 -> x0, waiting for transfers between devices: 71.3 us -> none  [shards(): lax.psum_scatter(weighted, 'ep', scatter_dimension=0, tiled=True)]
    pallas_call x0 -> x1, Pallas kernels: none -> 57.6 us  [shards(): pl.pallas_call(functools.partial(fused, devices, feature, width), out_sha...]
    all_gather x1 -> x0, blocking collectives: 23.7 us -> none  [shards(): gates_all = lax.all_gather(gates, 'ep', axis=0, tiled=True)]
    all_gather x1 -> x0, waiting for transfers between devices: 20.7 us -> none  [shards(): everything = lax.all_gather(tokens, 'ep', axis=0, tiled=True)]
    dot_general x2 -> x0, matrix products: 17.3 us -> none  [the longest x1 10 us: shards(): jnp.dot(everything, block[:, :2 * width], preferred_element_type=jnp.floa...]
    squeeze x1 -> x0, local copies, waits for them, and re-layouts: 7.91 us -> none  [shards(): block = expert_weights[0, :, :3 * width]]
  transfers between devices with their start and end apart: 2 -> 0, of which waited for: 2 -> 0; matrix products, arithmetic and copies ran while one was open for 7% -> 0% of each run, Pallas kernels for 0% -> 0%
where the time goes in v2:
time: 63 us; the launch traced here: 62.8 us
  Pallas kernels  57.6 us (91%)
  other arithmetic  4.22 us (7%)
  local copies, waits for them, and re-layouts  0.8 us (1%)
    pallas_call x1, Pallas kernels, shards(): pl.pallas_call(functools.partial(fused, devices, feature, width), out_sha...  57.6 us

profile of v2, /device:TPU:0, one launch (start us, length us, event | category | flops | bytes accessed | tf_op | source)
XLA Modules:
  0.0 62.8 jit_solution(6399497535795233495)
XLA Ops:
  0.0 0.8 %select_reduce_fusion = s32[16]{0:T(128)S(1)} fusion(s32[16]{0:T(128)} %param.10), kind=kLoop, calls=%fused_computation.15 | loop fusion | flops 752 | bytes 128 | tf_op jit(solution)/shard_map/reduce_sum | solution.py:14
  0.8 0.8 %convert_reduce_fusion = s32[16]{0:T(128)S(1)} fusion(s32[16]{0:T(128)} %param.11, s32[16]{0:T(128)S(1)} %select_reduce_fusion), kind=kLoop, calls=%fused_computation.14 | loop fusion | flops 752 | bytes 192 | tf_op jit(solution)/shard_map/reduce_sum | solution.py:15
  1.6 0.8 %compare_reduce_fusion = pred[64,16]{0,1:T(8,128)(4,1)S(1)} fusion(s32[64,8]{0,1:T(8,128)} %param.7, s32[16]{0:T(128)S(1)} %select_reduce_fusion), kind=kLoop, calls=%fused_computation.7 | loop fusion | flops 15360 | bytes 3136 | tf_op jit(solution)/shard_map/reduce_or | solution.py:19
  2.4 0.8 %fusion.4 = f32[64,16]{0,1:T(8,128)S(1)} fusion(f32[64,8]{0,1:T(8,128)} %param.8, s32[64,8]{0,1:T(8,128)} %param.7, s32[16]{0:T(128)S(1)} %select_reduce_fusion), kind=kLoop, calls=%fused_computation.8 | loop fusion | flops 23552 | bytes 8256 | tf_op jit(solution)/shard_map/reduce_sum | solution.py:18
  3.2 0.1 reduce-precision_convert_fusion
  3.3 0.1 pad_maximum_fusion
  3.3 0.1 copy.11
  3.4 1.0 %fusion.3 = bf16[64,2176]{1,0:T(8,128)(2,1)S(1)} fusion(bf16[64,32]{1,0:T(8,128)(2,1)S(1)} %copy.11, bf16[64,2048]{1,0:T(8,128)(2,1)} %param.6), kind=kLoop, calls=%fused_computation.5 | loop fusion | flops 835584 | bytes 544768 | tf_op jit(solution)/shard_map/concatenate | solution.py:251
  4.4 57.6 %shard_map.64 = bf16[2,32,2048]{2,1,0:T(8,128)(2,1)S(1)} custom-call(bf16[2,32,2176]{2,1,0:T(8,128)(2,1)S(1)} %bitcast.3, bf16[1,2048,3072]{2,1,0:T(8,128)(2,1)} %w_hbm.1), custom_call_target="tpu_custom_call" | custom-call | tf_op jit(solution)/shard_map/pallas_call | solution.py:255
  62.1 0.7 %copy.13 = bf16[64,2048]{1,0:T(8,128)(2,1)} copy(bf16[64,2048]{1,0:T(8,128)(2,1)S(1)} %bitcast.4) | data formatting | bytes 524288
  (1 shorter events, 0.0 us)

commit v3 on v1

v3 whole, which is shorter than its diff:
```python
import functools

import jax
import jax.numpy as jnp
from jax import lax
from jax.experimental import pallas as pl
from jax.experimental.pallas import tpu as pltpu
from jax.sharding import PartitionSpec as P


MESH = pl.DeviceIdType.MESH


def fused(devices, feature, width, capacity, home, spare, ids_hbm, gate_hbm, x_hbm, w_hbm, out_ref,
          xall, w, ids_ref, gate_ref, hid, part, sib_out, sib_in, near, back, in_sem, ga_send, ga_recv,
          sh_send, sh_recv, ex_send, ex_recv, re_send, re_recv):
    chips = devices // 2
    far = chips // 2
    me = lax.axis_index("ep")
    core = me % 2
    chip = me // 2
    odd = chip % 2
    place = (1 - odd) * (chip // 2) + odd * (chips - 1 - chip // 2)

    def device_at(spot):
        low = 1 - spot // far
        return 2 * (low * 2 * spot + (1 - low) * (2 * (chips - 1 - spot) + 1)) + core

    right = device_at((place + 1) % chips)
    left = device_at((place + chips - 1) % chips)
    sibling = me + 1 - 2 * core
    toward = (right, left)

    def remote(src, dst, send, recv, device):
        return pltpu.make_async_remote_copy(src_ref=src, dst_ref=dst, send_sem=send, recv_sem=recv,
                                            device_id={"ep": device}, device_id_type=MESH)

    def gather(kind, d, side):
        flip = 1 - side if kind == 1 and isinstance(d, int) and d == 0 else side
        first = 0 if isinstance(d, int) and d == 0 else kind * far
        return remote(xall.at[first + d, flip, core], xall.at[kind * far + d + 1, side, core],
                      ga_send.at[kind, d, side], ga_recv.at[kind, d + 1, side], toward[side])

    def share(block, side):
        slot = xall.at[block, side, core]
        return remote(slot, slot, sh_send.at[block, side], sh_recv.at[block, side], sibling)

    def exchange(block):
        return remote(sib_out.at[block % sib_out.shape[0]], sib_in.at[block],
                      ex_send.at[block], ex_recv.at[block], sibling)

    sums = (near, back)

    def reduce(kind, d, way):
        return remote(sums[kind].at[d, way], sums[kind].at[d - 1, way],
                      re_send.at[kind, d, way], re_recv.at[kind, d - 1, way], toward[1 - way])

    half_rows = x_hbm.shape[1]
    rows = 4 * half_rows

    def compute(block):
        for side in range(2):
            share(block, side).wait_recv()
        tile = 256

        @pl.loop(0, width // tile, unroll=True)
        def _(f):
            x = xall[block, :, :, :, :feature].reshape(rows, feature)
            at = pl.multiple_of(f * tile, tile)
            gate = jnp.dot(x, w[:, pl.ds(at, tile)], preferred_element_type=jnp.float32)
            lift = jnp.dot(x, w[:, pl.ds(width + at, tile)], preferred_element_type=jnp.float32)
            hid[:, pl.ds(at, tile)] = (gate * lax.logistic(gate) * lift).astype(jnp.bfloat16)

        extra = xall[block, :, :, :, feature:].reshape(rows, -1).astype(jnp.float32)
        gates = jnp.sum(jnp.where(at_home == me, extra, 0.0), axis=1, keepdims=True)
        ring = sib_out.shape[0]
        if 2 * far > ring:

            @pl.when(block >= ring)
            def _():
                exchange(block - ring).wait_send()

        span = 512

        @pl.loop(0, feature // span, unroll=True)
        def _(o):
            at = pl.multiple_of(o * span, span)
            answer = lax.dot_general(hid[...], w[pl.ds(at, span), 2 * width:],
                                     (((1,), (1,)), ((), ())), preferred_element_type=jnp.float32)
            answer = answer.astype(jnp.bfloat16).astype(jnp.float32)
            value = jnp.where(gates > 0, answer * gates, 0.0).reshape(2, 2, half_rows, span)
            mine = jnp.where(core == 0, value[:, 0], value[:, 1])
            other = jnp.where(core == 0, value[:, 1], value[:, 0])
            part[block, :, :, pl.ds(at, span)] = mine.astype(part.dtype)
            sib_out[block % ring, :, :, pl.ds(at, span)] = other.astype(jnp.bfloat16)

        exchange(block).start()

    def total(block, side):
        return part[block, side].astype(jnp.float32) + sib_in[block, side].astype(jnp.float32)

    def begin(kind, d):
        exchange(kind * far + d).wait_recv()
        for way in range(2):
            sums[kind][d, way] = total(kind * far + d, way).astype(jnp.bfloat16)
            reduce(kind, d, way).start()

    def pass_on(kind, d):
        exchange(kind * far + d).wait_recv()
        for way in range(2):
            reduce(kind, d + 1, way).wait_recv()
            held = sums[kind][d, way].astype(jnp.float32)
            sums[kind][d, way] = (total(kind * far + d, way) + held).astype(jnp.bfloat16)
            reduce(kind, d, way).start()

    fetches = [
        pltpu.make_async_copy(ids_hbm, ids_ref, in_sem.at[0]),
        pltpu.make_async_copy(gate_hbm, gate_ref, in_sem.at[1]),
        pltpu.make_async_copy(x_hbm, xall.at[0, :, core, :, pl.ds(0, feature)], in_sem.at[2]),
        pltpu.make_async_copy(w_hbm.at[0, :, pl.ds(0, 3 * width)], w, in_sem.at[3]),
    ]
    for fetch in fetches:
        fetch.start()
    barrier = pltpu.get_barrier_semaphore()
    for device in (right, left, sibling):
        pl.semaphore_signal(barrier, inc=1, device_id={"ep": device}, device_id_type=MESH)

    own_rows, lanes = ids_ref.shape[0], xall.shape[-1] - feature
    lane_row = lax.broadcasted_iota(jnp.int32, (1, lanes), 1)
    expert_row = jnp.where(lane_row < 2 * devices, lane_row % devices, -2)
    thirds = jnp.zeros((1, lanes), jnp.int32)
    at_home = jnp.full((1, lanes), -1, jnp.int32)
    for e in range(devices):
        thirds = thirds + jnp.where(expert_row == spare[e], 1, 0)
        at_home = jnp.where(expert_row == e, home[e], at_home)
    limit = capacity * jnp.where(thirds >= 6, 3, jnp.where(thirds >= 3, 2, 1))
    fetches[0].wait()
    fetches[1].wait()
    gates = jnp.zeros((own_rows, lanes), jnp.float32)
    for k in range(ids_ref.shape[1]):
        gates = gates + jnp.where(ids_ref[:, k : k + 1] == expert_row, gate_ref[:, k : k + 1], 0.0)
    named = jnp.where(gates > 0, 1.0, 0.0).astype(jnp.bfloat16)
    earlier = lax.broadcasted_iota(jnp.int32, (own_rows, own_rows), 1) < lax.broadcasted_iota(
        jnp.int32, (own_rows, own_rows), 0)
    arrival = jnp.dot(jnp.where(earlier, 1.0, 0.0).astype(jnp.bfloat16), named, preferred_element_type=jnp.float32)
    gates = jnp.where(arrival < limit.astype(jnp.float32), gates, 0.0)
    high = gates.astype(jnp.bfloat16)
    rest = gates - high.astype(jnp.float32)
    extra = jnp.where(lane_row < devices, high.astype(jnp.float32), rest).astype(jnp.bfloat16)
    xall[0, :, core, :, feature:] = extra.reshape(2, own_rows // 2, lanes)
    fetches[2].wait()
    pl.semaphore_wait(barrier, 3)

    for side in range(2):
        gather(0, 0, side).start()
    for side in range(2):
        share(0, side).start()
    fetches[3].wait()
    for side in range(2):
        gather(0, 0, side).wait_send()
    for side in range(2):
        gather(1, 0, side).start()

    @pl.loop(1, far + 1)
    def _(d):
        for side in range(2):
            gather(0, d - 1, side).wait_recv()

            @pl.when(d < far)
            def _():
                gather(0, d, side).start()

        for side in range(2):
            share(d, side).start()

        @pl.when(d == far - 1)
        def _():
            for side in range(2):
                gather(1, 0, side).wait_recv()
                gather(1, 1, side).start()
                share(far + 1, side).start()

        compute(d - 1)

    compute(far)

    @pl.loop(2, far)
    def _(d):
        for side in range(2):
            gather(1, d - 1, side).wait_recv()

            @pl.when(d < far - 1)
            def _():
                gather(1, d, side).start()

            share(far + d, side).start()

        @pl.when(d == 2)
        def _():
            begin(0, far)

        compute(far + d - 1)

    pass_on(0, far - 1)
    compute(2 * far - 1)
    begin(1, far - 1)

    @pl.loop(2, far)
    def _(step):
        pass_on(0, far - step)
        pass_on(1, far - step)

    exchange(0).wait_recv()
    for half in range(2):
        reduce(0, 1, half).wait_recv()
        reduce(1, 1, 1 - half).wait_recv()
        out_ref[half] = (total(0, half) + near[0, half].astype(jnp.float32)
                         + back[0, 1 - half].astype(jnp.float32)).astype(out_ref.dtype)

    @pl.loop(0, 2 * far)
    def _(block):
        for side in range(2):
            share(block, side).wait_send()

    @pl.loop(max(0, 2 * far - sib_out.shape[0]), 2 * far)
    def _(block):
        exchange(block).wait_send()

    for side in range(2):
        gather(1, 0, side).wait_send()
        gather(0, far - 1, side).wait_send()
        reduce(0, far, side).wait_send()
        reduce(0, far - 1, side).wait_send()
        reduce(1, far - 1, side).wait_send()

    @pl.loop(1, far - 1)
    def _(d):
        for side in range(2):
            for kind in range(2):
                gather(kind, d, side).wait_send()
                reduce(kind, d, side).wait_send()


def shards(tokens, expert_ids, gate_values, expert_weights, home_slot, spare_expert):
    devices = lax.axis_size("ep")
    local_tokens, feature = tokens.shape
    capacity = local_tokens * expert_ids.shape[1] // devices
    width = expert_weights.shape[2] // 4
    half_rows = local_tokens // 2
    lanes = pl.cdiv(2 * devices, 128) * 128
    x = tokens.reshape(2, half_rows, feature)
    far = devices // 4
    kept = jnp.float32 if devices <= 16 else jnp.bfloat16
    dma = pltpu.SemaphoreType.DMA
    result = pl.pallas_call(
        functools.partial(fused, devices, feature, width, capacity),
        out_shape=jax.ShapeDtypeStruct((2, half_rows, feature), jnp.bfloat16),
        in_specs=[pl.BlockSpec(memory_space=pltpu.SMEM)] * 2 + [pl.BlockSpec(memory_space=pl.ANY)] * 4,
        out_specs=pl.BlockSpec(memory_space=pltpu.VMEM),
        scratch_shapes=[
            pltpu.VMEM((2 * far, 2, 2, half_rows, feature + lanes), jnp.bfloat16),
            pltpu.VMEM((feature, 3 * width), jnp.bfloat16),
            pltpu.VMEM(expert_ids.shape, jnp.int32),
            pltpu.VMEM(gate_values.shape, jnp.float32),
            pltpu.VMEM((2 * local_tokens, width), jnp.bfloat16),
            pltpu.VMEM((2 * far, 2, half_rows, feature), kept),
            pltpu.VMEM((8, 2, half_rows, feature), jnp.bfloat16),
            pltpu.VMEM((2 * far, 2, half_rows, feature), jnp.bfloat16),
            pltpu.VMEM((far + 1, 2, half_rows, feature), jnp.bfloat16),
            pltpu.VMEM((far, 2, half_rows, feature), jnp.bfloat16),
            dma((4,)),
            dma((2, far + 1, 2)),
            dma((2, far + 1, 2)),
            dma((2 * far, 2)),
            dma((2 * far, 2)),
            dma((2 * far,)),
            dma((2 * far,)),
            dma((2, far + 1, 2)),
            dma((2, far + 1, 2)),
        ],
        compiler_params=pltpu.CompilerParams(
            collective_id=0, has_side_effects=True, vmem_limit_bytes=(44 if devices <= 16 else 62) * 2**20
        ),
    )(home_slot, spare_expert, expert_ids, gate_values, x, expert_weights)
    return result.reshape(local_tokens, feature)


def solution(mesh):
    in_specs = (
        P(("groups", "ep"), None),
        P(("groups", "ep"), None),
        P(("groups", "ep"), None),
        P(("groups", "ep"), None, None),
        P("groups"),
        P("groups"),
    )
    out_specs = P(("groups", "ep"), None)
    return jax.shard_map(shards, mesh=mesh, in_specs=in_specs, out_specs=out_specs, check_vma=False)
```

time: 159 us -> 61.7 us (0.39)
  waiting for transfers between devices: 92.8 us -> 0 us
  Pallas kernels: 0 us -> 56.9 us
  blocking collectives: 23.7 us -> 0 us
  matrix products: 17.4 us -> 0 us
  between operations: 13.4 us -> 0.01 us
  local copies, waits for them, and re-layouts: 8.05 us -> 4.5 us
  other arithmetic: 3.21 us -> 0 us
    reduce_scatter x1 -> x0, waiting for transfers between devices: 71.3 us -> none  [shards(): lax.psum_scatter(weighted, 'ep', scatter_dimension=0, tiled=True)]
    pallas_call x0 -> x1, Pallas kernels: none -> 56.9 us  [shards(): pl.pallas_call(functools.partial(fused, devices, feature, width, capacity...]
    all_gather x1 -> x0, blocking collectives: 23.7 us -> none  [shards(): gates_all = lax.all_gather(gates, 'ep', axis=0, tiled=True)]
    all_gather x1 -> x0, waiting for transfers between devices: 20.7 us -> none  [shards(): everything = lax.all_gather(tokens, 'ep', axis=0, tiled=True)]
    dot_general x3 -> x0, matrix products: 17.4 us -> none  [the longest x1 10 us: shards(): jnp.dot(everything, block[:, :2 * width], preferred_element_type=jnp.floa...]
    squeeze x1 -> x0, local copies, waits for them, and re-layouts: 7.91 us -> none  [shards(): block = expert_weights[0, :, :3 * width]]
    unnamed x1 -> x9, local copies, waits for them, and re-layouts: 0.1 us -> 4.5 us
    reduce_sum x3 -> x0, other arithmetic: 2.4 us -> none  [the longest x1 0.84 us: device_gates(): jnp.sum((spare_expert[None, :] == expert_of[:, None]).astype(jnp.int32),...]
  transfers between devices with their start and end apart: 2 -> 0, of which waited for: 2 -> 0; matrix products, arithmetic and copies ran while one was open for 7% -> 0% of each run, Pallas kernels for 0% -> 0%
where the time goes in v3:
time: 61.7 us; the launch traced here: 61.4 us
  Pallas kernels  56.9 us (92%)
  local copies, waits for them, and re-layouts  4.5 us (7%)
    pallas_call x1, Pallas kernels, shards(): pl.pallas_call(functools.partial(fused, devices, feature, width, capacity...  56.9 us
    unnamed x9, local copies, waits for them, and re-layouts  4.5 us

profile of v3, /device:TPU:0, one launch (start us, length us, event | category | flops | bytes accessed | tf_op | source)
XLA Modules:
  0.0 61.4 jit_solution(16644924748253892666)
XLA Ops:
  0.0 0.8 %copy.7.ids_hbm = s32[64,8]{1,0:T(8,128)S(1)} copy(s32[64,8]{0,1:T(8,128)} %param.7) | data formatting | bytes 4096 | tf_op args[1]
  0.8 0.8 %copy.8.gate_hbm = f32[64,8]{1,0:T(8,128)S(1)} copy(f32[64,8]{0,1:T(8,128)} %param.8) | data formatting | bytes 4096 | tf_op args[2]
  1.5 0.0 copy-start
  1.5 0.9 %copy-done = bf16[64,2048]{1,0:T(8,128)(2,1)S(1)} copy-done((bf16[64,2048]{1,0:T(8,128)(2,1)S(1)}, bf16[64,2048]{1,0:T(8,128)(2,1)}, u32[]{:S(2)}) %copy-start) | copy-done | bytes 262168
  2.5 0.0 copy-start.1
  2.5 0.7 %copy-done.1 = s32[16]{0:T(128)S(1)} copy-done((s32[16]{0:T(128)S(1)}, s32[16]{0:T(128)}, u32[]{:S(2)}) %copy-start.1) | copy-done | bytes 88
  3.1 0.0 copy-start.2
  3.1 0.7 %copy-done.2 = s32[16]{0:T(128)S(1)} copy-done((s32[16]{0:T(128)S(1)}, s32[16]{0:T(128)}, u32[]{:S(2)}) %copy-start.2) | copy-done | bytes 88
  3.8 56.9 %shard_map.64 = bf16[2,32,2048]{2,1,0:T(8,128)(2,1)S(1)} custom-call(s32[16]{0:T(128)S(1)} %copy-done.1, s32[16]{0:T(128)S(1)} %copy-done.2, s32[64,8]{1,0:T(8,128)S(1)} %copy.7.ids_hbm, f32[64,8]{1,0:T(8,128)S(1)} %copy.8.gate_hbm, bf16[2,32,2048]{2,1,0:T(8,128)(2,1)S(1)} %bitcast.3, bf16[1,2048,3072]{2,1,0:T(8,128)(2,1)} %w_hbm.1), custom_call_target="tpu_custom_call" | custom-call | tf_op jit(solution)/shard_map/pallas_call | solution.py:255
  60.7 0.7 %copy.10 = bf16[64,2048]{1,0:T(8,128)(2,1)} copy(bf16[64,2048]{1,0:T(8,128)(2,1)S(1)} %bitcast.2) | data formatting | bytes 524288
Async XLA Ops:
  1.5 0.9 %copy-start = (bf16[64,2048]{1,0:T(8,128)(2,1)S(1)}, bf16[64,2048]{1,0:T(8,128)(2,1)}, u32[]{:S(2)}) copy-start(bf16[64,2048]{1,0:T(8,128)(2,1)} %param.6) | copy-start | bytes 786436
  2.5 0.7 %copy-start.1 = (s32[16]{0:T(128)S(1)}, s32[16]{0:T(128)}, u32[]{:S(2)}) copy-start(s32[16]{0:T(128)} %home.1) | copy-start | bytes 196
  3.1 0.7 %copy-start.2 = (s32[16]{0:T(128)S(1)}, s32[16]{0:T(128)}, u32[]{:S(2)}) copy-start(s32[16]{0:T(128)} %spare.1) | copy-start | bytes 196

commit v4 on v3

--- a/solution.py
+++ b/solution.py
@@ -63,7 +63,7 @@
             share(block, side).wait_recv()
         tile = 256
 
-        @pl.loop(0, width // tile, unroll=True)
+        @pl.loop(0, width // tile)
         def _(f):
             x = xall[block, :, :, :, :feature].reshape(rows, feature)
             at = pl.multiple_of(f * tile, tile)
@@ -82,7 +82,7 @@
 
         span = 512
 
-        @pl.loop(0, feature // span, unroll=True)
+        @pl.loop(0, feature // span)
         def _(o):
             at = pl.multiple_of(o * span, span)
             answer = lax.dot_general(hid[...], w[pl.ds(at, span), 2 * width:],
@@ -125,7 +125,7 @@
     for device in (right, left, sibling):
         pl.semaphore_signal(barrier, inc=1, device_id={"ep": device}, device_id_type=MESH)
 
-    own_rows, lanes = ids_ref.shape[0], xall.shape[-1] - feature
+    own_rows, lanes = ids_ref.shape[1], xall.shape[-1] - feature
     lane_row = lax.broadcasted_iota(jnp.int32, (1, lanes), 1)
     expert_row = jnp.where(lane_row < 2 * devices, lane_row % devices, -2)
     thirds = jnp.zeros((1, lanes), jnp.int32)
@@ -137,8 +137,9 @@
     fetches[0].wait()
     fetches[1].wait()
     gates = jnp.zeros((own_rows, lanes), jnp.float32)
-    for k in range(ids_ref.shape[1]):
-        gates = gates + jnp.where(ids_ref[:, k : k + 1] == expert_row, gate_ref[:, k : k + 1], 0.0)
+    ids, weights = ids_ref[...].T, gate_ref[...].T
+    for k in range(ids.shape[1]):
+        gates = gates + jnp.where(ids[:, k : k + 1] == expert_row, weights[:, k : k + 1], 0.0)
     named = jnp.where(gates > 0, 1.0, 0.0).astype(jnp.bfloat16)
     earlier = lax.broadcasted_iota(jnp.int32, (own_rows, own_rows), 1) < lax.broadcasted_iota(
         jnp.int32, (own_rows, own_rows), 0)
@@ -260,8 +261,8 @@
         scratch_shapes=[
             pltpu.VMEM((2 * far, 2, 2, half_rows, feature + lanes), jnp.bfloat16),
             pltpu.VMEM((feature, 3 * width), jnp.bfloat16),
-            pltpu.VMEM(expert_ids.shape, jnp.int32),
-            pltpu.VMEM(gate_values.shape, jnp.float32),
+            pltpu.VMEM(expert_ids.shape[::-1], jnp.int32),
+            pltpu.VMEM(gate_values.shape[::-1], jnp.float32),
             pltpu.VMEM((2 * local_tokens, width), jnp.bfloat16),
             pltpu.VMEM((2 * far, 2, half_rows, feature), kept),
             pltpu.VMEM((8, 2, half_rows, feature), jnp.bfloat16),
@@ -279,9 +280,9 @@
             dma((2, far + 1, 2)),
         ],
         compiler_params=pltpu.CompilerParams(
-            collective_id=0, has_side_effects=True, vmem_limit_bytes=(44 if devices <= 16 else 62) * 2**20
+            collective_id=0, has_side_effects=True, vmem_limit_bytes=63 * 2**20
         ),
-    )(home_slot, spare_expert, expert_ids, gate_values, x, expert_weights)
+    )(home_slot, spare_expert, expert_ids.T, gate_values.T, x, expert_weights)
     return result.reshape(local_tokens, feature)
 
 

time: 61.7 us -> 63.6 us (1.031)
  Pallas kernels: 56.9 us -> 61.8 us
  local copies, waits for them, and re-layouts: 4.5 us -> 1.67 us
    pallas_call x1, Pallas kernels: 56.9 us -> 61.8 us  [shards(): pl.pallas_call(functools.partial(fused, devices, feature, width, capacity...]
    unnamed x9 -> x1, local copies, waits for them, and re-layouts: 4.5 us -> 1.67 us
where the time goes in v4:
time: 63.6 us; the launch traced here: 63.4 us
  Pallas kernels  61.8 us (97%)
  local copies, waits for them, and re-layouts  1.67 us (3%)
    pallas_call x1, Pallas kernels, shards(): pl.pallas_call(functools.partial(fused, devices, feature, width, capacity...  61.8 us
    unnamed x1, local copies, waits for them, and re-layouts  1.67 us

profile of v4, /device:TPU:0, one launch (start us, length us, event | category | flops | bytes accessed | tf_op | source)
XLA Modules:
  0.0 63.4 jit_solution(10094596322474956056)
XLA Ops:
  0.0 61.8 %shard_map.64 = bf16[2,32,2048]{2,1,0:T(8,128)(2,1)} custom-call(s32[16]{0:T(128)} %home.1, s32[16]{0:T(128)} %spare.1, s32[8,64]{1,0:T(8,128)} %bitcast.6, f32[8,64]{1,0:T(8,128)} %bitcast.7, bf16[2,32,2048]{2,1,0:T(8,128)(2,1)} %bitcast.5, bf16[1,2048,3072]{2,1,0:T(8,128)(2,1)} %w_hbm.1), custom_call_target="tpu_custom_call" | custom-call | tf_op jit(solution)/shard_map/pallas_call | solution.py:256
  61.8 1.7 %copy.8 = bf16[64,2048]{1,0:T(8,128)(2,1)} copy(bf16[64,2048]{1,0:T(8,128)(2,1)} %bitcast.4) | data formatting | bytes 524288
